TPU v7x, 32 devices: a whole 2x2x4 slice. The times are simulated.
32 devices in a mesh: seq: 16 (over z, y, core), dp: 2 (over x).
Axes of the slice: x: 2, y: 2, z: 4, core: 2. Of those that a mesh axis runs over, the one named last changes fastest.
Arguments:
- tokens: bfloat16 [2, 4096, 4096], P('dp', 'seq'), may hold values from -6 to 6
- query: bfloat16 [2, 4096, 2048], P('dp', 'seq'), may hold values from -5 to 5
- key: bfloat16 [2, 4096, 2048], P('dp', 'seq'), may hold values from -5 to 5
- value: bfloat16 [2, 4096, 2048], P('dp', 'seq'), may hold values from -6 to 6
- output_gradient: bfloat16 [2, 4096, 2048], P('dp', 'seq'), may hold values from -24 to 24
- adapter_down_weight: bfloat16 [3, 8, 4096], replicated, may hold values from -0.09375 to 0.09375
- adapter_up_weight: bfloat16 [3, 8, 2048], replicated, may hold values from -2 to 2
Outputs:
- grad_query: bfloat16 [2, 4096, 2048], P('dp', 'seq')
- grad_key: bfloat16 [2, 4096, 2048], P('dp', 'seq')
- grad_value: bfloat16 [2, 4096, 2048], P('dp', 'seq')
- grad_down: float32 [3, 8, 4096], replicated
- grad_up: float32 [3, 8, 2048], replicated
All inputs are finite; a program needn't handle non-finite values.
Results may differ from a plain program's by a relative error of at most 0.011.
Values may be sent and summed in bfloat16 or wider, within the bound.
A program may use at most 64 MiB of HBM per device.

v0:
```python
import math

import jax
import jax.numpy as jnp
from jax import lax
from jax.sharding import PartitionSpec as P

SHIFTED_HEADS = 16
HEAD_FEATURES = 128


adapter_scale = 2.0


def shifted_2(shard, axis, by):
    peers = lax.axis_size(axis)
    return lax.ppermute(shard, axis, [(i, (i + by) % peers) for i in range(peers)])


def attend_back(query, key, value, output_gradient, allowed):
    scale_factor = 1.0 / math.sqrt(query.shape[-1])
    scores = (
        jnp.einsum("qhd,khd->hqk", query, key, preferred_element_type=jnp.float32) * scale_factor
    )
    scores = jnp.where(allowed[None], scores, -jnp.inf)
    highest = jnp.max(scores, axis=-1, keepdims=True)
    raised = jnp.exp(scores - highest)
    weights = raised / jnp.sum(raised, axis=-1, keepdims=True)
    weights_low = weights.astype(jnp.bfloat16)
    attended = jnp.einsum("hqk,khd->qhd", weights_low, value, preferred_element_type=jnp.float32)
    row_dots = jnp.sum(output_gradient.astype(jnp.float32) * attended, axis=-1)
    grad_value = jnp.einsum(
        "hqk,qhd->khd", weights_low, output_gradient, preferred_element_type=jnp.float32
    )
    grad_weights = jnp.einsum(
        "qhd,khd->hqk", output_gradient, value, preferred_element_type=jnp.float32
    )
    grad_scores = (weights * (grad_weights - row_dots.T[:, :, None])).astype(jnp.bfloat16)
    grad_query = (
        jnp.einsum("hqk,khd->qhd", grad_scores, key, preferred_element_type=jnp.float32)
        * scale_factor
    )
    grad_key = (
        jnp.einsum("hqk,qhd->khd", grad_scores, query, preferred_element_type=jnp.float32)
        * scale_factor
    )
    return (grad_query, grad_key, grad_value)


def shards(tokens, query, key, value, output_gradient, adapter_down_weight, adapter_up_weight):
    batch, rows, width = query.shape
    half_heads = SHIFTED_HEADS // 2
    half_rows = rows // 2
    backward = jax.vmap(attend_back, in_axes=(0, 0, 0, 0, None))
    causal = jnp.arange(rows)[:, None] >= jnp.arange(rows)[None, :]
    query_heads = query.reshape(batch, rows, SHIFTED_HEADS, HEAD_FEATURES)
    key_heads = key.reshape(batch, rows, SHIFTED_HEADS, HEAD_FEATURES)
    value_heads = value.reshape(batch, rows, SHIFTED_HEADS, HEAD_FEATURES)
    grad_heads = output_gradient.reshape(batch, rows, SHIFTED_HEADS, HEAD_FEATURES)
    plain = backward(
        query_heads[:, :, :half_heads],
        key_heads[:, :, :half_heads],
        value_heads[:, :, :half_heads],
        grad_heads[:, :, :half_heads],
        causal,
    )
    moved_query = query_heads[:, :, half_heads:]
    moved_key = key_heads[:, :, half_heads:]
    moved_value = value_heads[:, :, half_heads:]
    moved_grad = grad_heads[:, :, half_heads:]
    next_query, next_key, next_value, next_grad = shifted_2(
        (
            moved_query[:, :half_rows],
            moved_key[:, :half_rows],
            moved_value[:, :half_rows],
            moved_grad[:, :half_rows],
        ),
        "seq",
        -1,
    )
    group = backward(
        jnp.concatenate([moved_query[:, half_rows:], next_query], axis=1),
        jnp.concatenate([moved_key[:, half_rows:], next_key], axis=1),
        jnp.concatenate([moved_value[:, half_rows:], next_value], axis=1),
        jnp.concatenate([moved_grad[:, half_rows:], next_grad], axis=1),
        causal,
    )
    lower = [part[:, half_rows:].astype(jnp.bfloat16) for part in group]
    ret_query, ret_key, ret_value = shifted_2((lower[0], lower[1], lower[2]), "seq", 1)
    shifted = (
        jnp.concatenate([ret_query, group[0][:, :half_rows].astype(jnp.bfloat16)], axis=1),
        jnp.concatenate([ret_key, group[1][:, :half_rows].astype(jnp.bfloat16)], axis=1),
        jnp.concatenate([ret_value, group[2][:, :half_rows].astype(jnp.bfloat16)], axis=1),
    )
    grads = [
        jnp.concatenate(
            [plain[projection_index].astype(jnp.bfloat16), shifted[projection_index]], axis=2
        ).reshape(batch, rows, width)
        for projection_index in range(3)
    ]
    flattened_tokens = tokens.reshape(batch * rows, tokens.shape[2])
    stacked_gradients = jnp.stack(grads).reshape(3, batch * rows, width)
    down_projected = jnp.einsum(
        "uy,hfy->huf", flattened_tokens, adapter_down_weight, preferred_element_type=jnp.float32
    ).astype(jnp.bfloat16)
    returned_values = jnp.einsum(
        "kbv,kcv->kbc", stacked_gradients, adapter_up_weight, preferred_element_type=jnp.float32
    ).astype(jnp.bfloat16)
    down_sum = jnp.einsum(
        "pnr,nd->prd", returned_values, flattened_tokens, preferred_element_type=jnp.float32
    )
    up_sum = jnp.einsum(
        "pnr,pnh->prh", down_projected, stacked_gradients, preferred_element_type=jnp.float32
    )
    down_sum, up_sum = lax.psum((down_sum, up_sum), ("seq", "dp"))
    total_gradient = batch * rows * lax.axis_size("seq") * lax.axis_size("dp")
    scale_factor = adapter_scale / math.sqrt(total_gradient)
    return (grads[0], grads[1], grads[2], down_sum * scale_factor, up_sum * scale_factor)


def solution(mesh):
    in_specs = (
        P("dp", "seq", None),
        P("dp", "seq", None),
        P("dp", "seq", None),
        P("dp", "seq", None),
        P("dp", "seq", None),
        P(),
        P(),
    )
    out_specs = (P("dp", "seq", None), P("dp", "seq", None), P("dp", "seq", None), P(), P())
    return jax.shard_map(shards, mesh=mesh, in_specs=in_specs, out_specs=out_specs, check_vma=False)
```

profile of v0, /device:TPU:0, one launch (start us, length us, event | category | flops | bytes accessed | tf_op | source)
XLA Modules:
  0.0 231.5 jit_solution(3163128346158799110)
XLA Ops:
  7.2 1.6 copy.38
  8.9 1.0 fusion.64
  9.8 1.8 copy.107
  11.6 5.4 %collective-permute-start.1 = (bf16[1,128,8,128]{3,1,2,0:T(8,128)(2,1)}, bf16[1,128,8,128]{3,1,2,0:T(8,128)(2,1)}, u32[]{:S(2)}, u32[]{:S(2)}) collective-permute-start(bf16[1,128,8,128]{3,1,2,0:T(8,128)(2,1)} %copy.107), channel_id=1, source_target_pairs={{0,30},{2,0},{4,2},{6,4},{8,6},{10,8},{12,10},{14,12},{16,14},{18,... | collective-permute-start | bytes 786440 | tf_op jit(solution)/shard_map/ppermute | solution.py:17
  17.1 2.3 copy.40
  19.3 1.9 fusion.63
  21.2 1.8 copy.105
  23.0 0.7 collective-permute-start
  23.7 1.5 copy.44
  25.2 1.1 fusion.66
  26.3 1.8 copy.111
  28.1 1.5 copy.42
  29.5 0.9 fusion.65
  30.5 1.8 copy.109
  32.9 0.8 slice.92
  33.8 2.0 copy.102
  35.8 3.4 %fusion.71 = (f32[8,256]{1,0:T(8,128)S(1)}, f32[8,256,256]{1,2,0:T(8,128)}) fusion(pred[256,256]{0,1:T(8,128)(4,1)S(1)} %iota_compare_fusion, bf16[1,256,16,128]{1,3,2,0:T(8,128)(2,1)} %bitcast.180, bf16[1,256,16,128]{1,3,2,0:T(8,128)(2,1)} %bitcast.177), kind=kOutput, calls=%fused_computation.92 | convolution fusion | flops 136315136 | bytes 3219456 | tf_op jit(solution)/shard_map/vmap()/sub | solution.py:27
  39.2 3.0 %fusion.16 = bf16[1,256,8,128]{1,3,2,0:T(8,128)(2,1)} fusion(bf16[1,256,16,128]{1,3,2,0:T(8,128)(2,1)S(1)} %bitcast.174, f32[8,256,256]{1,2,0:T(8,128)} %get-tuple-element.34, f32[8,256]{1,0:T(8,128)S(1)} %get-tuple-element.33), kind=kOutput, calls=%fused_computation.31 | convolution fusion | flops 135528448 | bytes 3153920 | tf_op jit(solution)/shard_map/vmap(hqk,qhd->khd)/dot_general | solution.py:32
  43.5 1.0 copy-done.2
  44.4 1.1 fusion.18
  45.5 0.8 copy.106
  46.4 1.9 copy.104
  48.2 1.8 copy.110
  50.0 1.8 copy.108
  51.8 2.3 fusion.20
  54.2 3.3 %fusion.70 = (f32[8,256]{1,0:T(8,128)S(1)}, f32[8,256,256]{1,2,0:T(8,128)}) fusion(pred[256,256]{0,1:T(8,128)(4,1)S(1)} %iota_compare_fusion, bf16[1,128,8,128]{3,1,2,0:T(8,128)(2,1)} %collective-permute-done, bf16[1,128,8,128]{3,1,2,0:T(8,128)(2,1)} %copy.104, bf16[1,128,8,128]{3,1,2,0:T(8,128)(2,1)} %collective-permute-done.1, ...), kind=kOutput, calls=%fused_computation.91 | convolution fusion | flops 138412288 | bytes 3219456 | tf_op jit(solution)/shard_map/vmap()/sub | solution.py:27
  57.5 2.5 %multiply_reduce_fusion = f32[256,8]{0,1:T(8,128)S(1)} fusion(bf16[1,128,8,128]{3,1,2,0:T(8,128)(2,1)} %collective-permute-done.3, bf16[1,128,8,128]{3,1,2,0:T(8,128)(2,1)S(1)} %copy-done.14, bf16[1,128,8,128]{3,1,2,0:T(8,128)(2,1)} %collective-permute-done.2, bf16[1,128,8,128]{3,1,2,0:T(8,128)(2,1)S(1)} %copy-done.13, ...), kind=kOutput, calls=%fused_computation.42 | convolution fusion | flops 137885696 | bytes 3162112 | tf_op jit(solution)/shard_map/vmap(hqk,khd->qhd)/dot_general | solution.py:30
  59.9 1.5 multiply_convert_fusion
  61.5 1.3 fusion.21
  62.9 1.4 fusion.19
  64.4 0.8 fusion.68
  65.2 1.6 collective-permute-start.4
  66.9 1.5 fusion.17
  68.3 0.9 fusion.67
  69.3 7.4 %collective-permute-done.4 = bf16[1,128,8,128]{1,3,2,0:T(8,128)(2,1)S(1)} collective-permute-done((bf16[1,128,8,128]{1,3,2,0:T(8,128)(2,1)S(1)}, bf16[1,128,8,128]{1,3,2,0:T(8,128)(2,1)S(1)}, u32[]{:S(2)}, u32[]{:S(2)}) %collective-permute-start.4) | collective-permute-done | bytes 262176 | tf_op jit(solution)/shard_map/ppermute | solution.py:17
  76.8 1.4 copy.74
  78.3 2.2 maximum_maximum_fusion.1
  80.5 2.3 copy.75
  82.8 2.2 maximum_maximum_fusion.2
  85.0 2.3 copy.76
  87.3 4.5 %fusion.13 = f32[3,8,2048]{2,1,0:T(8,128)} fusion(bf16[1,1,256,2048]{3,2,0,1:T(8,128)(2,1)} %copy.76, bf16[1,1,256,2048]{3,2,0,1:T(8,128)(2,1)} %copy.75, bf16[1,1,256,2048]{3,2,0,1:T(8,128)(2,1)} %copy.74, bf16[3,8,4096]{2,1,0:T(8,128)(2,1)S(1)} %copy-done.15, bf16[1,256,4096]{2,1,0:T(8,128)(2,1)S(1)} %copy-done), kind=kOutput, calls=%fused_computation.28 | convolution fusion | flops 78649344 | bytes 5636096 | tf_op jit(solution)/shard_map/pnr,pnh->prh/dot_general | solution.py:112
  91.8 4.4 %fusion.4 = f32[3,8,4096]{2,1,0:T(8,128)} fusion(bf16[1,256,4096]{2,1,0:T(8,128)(2,1)S(1)} %copy-done, bf16[3,8,2048]{2,1,0:T(8,128)(2,1)S(1)} %copy-done.16, bf16[1,1,256,2048]{3,2,0,1:T(8,128)(2,1)} %copy.76, bf16[1,1,256,2048]{3,2,0,1:T(8,128)(2,1)} %copy.75, bf16[1,1,256,2048]{3,2,0,1:T(8,128)(2,1)} %copy.74), kind=kOutput, calls=%fused_computation.5 | convolution fusion | flops 78649344 | bytes 5734400 | tf_op jit(solution)/shard_map/pnr,nd->prd/dot_general | solution.py:109
  96.2 1.4 copy.77
  97.7 2.4 %copy.78 = bf16[1,256,2048]{2,1,0:T(8,128)(2,1)} copy(bf16[1,256,2048]{1,2,0:T(8,128)(2,1)} %bitcast.169) | data formatting | bytes 2097152
  100.0 1.4 copy.79
  101.4 119.9 %all-reduce.3.cloned.1.call-done = (f32[3,8,4096]{2,1,0:T(8,128)}, f32[3,8,2048]{2,1,0:T(8,128)}) async-done(((f32[3,8,4096]{2,1,0:T(8,128)}, f32[3,8,2048]{2,1,0:T(8,128)}), (f32[3,8,4096]{2,1,0:T(8,128)}, f32[3,8,2048]{2,1,0:T(8,128)})) %all-reduce.3.cloned.1.call-update) | async-done | bytes 589840 | tf_op jit(solution)/shard_map/psum | solution.py:115
  221.3 1.8 broadcast_multiply_fusion
  223.1 1.6 broadcast_multiply_fusion.1
  (54 shorter events, 2.3 us)
Async XLA Ops:
  7.2 80.1 %copy-start = (bf16[1,256,4096]{2,1,0:T(8,128)(2,1)S(1)}, bf16[1,256,4096]{2,1,0:T(8,128)(2,1)}, u32[]{:S(2)}) copy-start(bf16[1,256,4096]{2,1,0:T(8,128)(2,1)} %param.7) | copy-start | bytes 6291460
  7.2 214.1 %all-reduce.3.cloned.1.call-start = ((), (), s32[]{:S(2)}) async-start(), calls=%async_computation | async-start | bytes 1179648 | tf_op jit(solution)/shard_map/psum | solution.py:115
  8.9 12.4 %copy-start.4 = (bf16[1,256,2048]{1,2,0:T(8,128)(2,1)}, bf16[1,256,2048]{1,2,0:T(8,128)(2,1)S(1)}, u32[]{:S(2)}) copy-start(bf16[1,256,2048]{1,2,0:T(8,128)(2,1)S(1)} %copy.38) | copy-start | bytes 3145732
  11.6 42.5 %collective-permute-start.1 = (bf16[1,128,8,128]{3,1,2,0:T(8,128)(2,1)}, bf16[1,128,8,128]{3,1,2,0:T(8,128)(2,1)}, u32[]{:S(2)}, u32[]{:S(2)}) collective-permute-start(bf16[1,128,8,128]{3,1,2,0:T(8,128)(2,1)} %copy.107), channel_id=1, source_target_pairs={{0,30},{2,0},{4,2},{6,4},{8,6},{10,8},{12,10},{14,12},{16,14},{18,... | collective-permute-start | bytes 786440 | tf_op jit(solution)/shard_map/ppermute | solution.py:17
  23.0 31.1 %collective-permute-start = (bf16[1,128,8,128]{3,1,2,0:T(8,128)(2,1)}, bf16[1,128,8,128]{3,1,2,0:T(8,128)(2,1)}, u32[]{:S(2)}, u32[]{:S(2)}) collective-permute-start(bf16[1,128,8,128]{3,1,2,0:T(8,128)(2,1)} %copy.105), channel_id=1, source_target_pairs={{0,30},{2,0},{4,2},{6,4},{8,6},{10,8},{12,10},{14,12},{16,14},{18,... | collective-permute-start | bytes 786440 | tf_op jit(solution)/shard_map/ppermute | solution.py:17
  25.2 2.9 %copy-start.6 = (bf16[1,256,2048]{1,2,0:T(8,128)(2,1)}, bf16[1,256,2048]{1,2,0:T(8,128)(2,1)S(1)}, u32[]{:S(2)}) copy-start(bf16[1,256,2048]{1,2,0:T(8,128)(2,1)S(1)} %copy.44) | copy-start | bytes 3145732
  28.1 29.4 %collective-permute-start.3 = (bf16[1,128,8,128]{3,1,2,0:T(8,128)(2,1)}, bf16[1,128,8,128]{3,1,2,0:T(8,128)(2,1)}, u32[]{:S(2)}, u32[]{:S(2)}) collective-permute-start(bf16[1,128,8,128]{3,1,2,0:T(8,128)(2,1)} %copy.111), channel_id=1, source_target_pairs={{0,30},{2,0},{4,2},{6,4},{8,6},{10,8},{12,10},{14,12},{16,14},{18,... | collective-permute-start | bytes 786440 | tf_op jit(solution)/shard_map/ppermute | solution.py:17
  32.3 25.1 %collective-permute-start.2 = (bf16[1,128,8,128]{3,1,2,0:T(8,128)(2,1)}, bf16[1,128,8,128]{3,1,2,0:T(8,128)(2,1)}, u32[]{:S(2)}, u32[]{:S(2)}) collective-permute-start(bf16[1,128,8,128]{3,1,2,0:T(8,128)(2,1)} %copy.109), channel_id=1, source_target_pairs={{0,30},{2,0},{4,2},{6,4},{8,6},{10,8},{12,10},{14,12},{16,14},{18,... | collective-permute-start | bytes 786440 | tf_op jit(solution)/shard_map/ppermute | solution.py:17
  39.2 3.0 %copy-start.7 = (bf16[1,256,2048]{1,2,0:T(8,128)(2,1)S(1)}, bf16[1,256,2048]{1,2,0:T(8,128)(2,1)}, u32[]{:S(2)}) copy-start(bf16[1,256,2048]{1,2,0:T(8,128)(2,1)} %copy-done.6) | copy-start | bytes 3145732
  39.2 3.0 %copy-start.12 = (bf16[1,256,8,128]{3,1,2,0:T(8,128)(2,1)S(1)}, bf16[1,256,8,128]{3,1,2,0:T(8,128)(2,1)}, u32[]{:S(2)}) copy-start(bf16[1,256,8,128]{3,1,2,0:T(8,128)(2,1)} %copy.102) | copy-start | bytes 1572868
  39.2 3.0 %copy-start.17 = (f32[8,256,256]{1,2,0:T(8,128)S(1)}, f32[8,256,256]{1,2,0:T(8,128)}, u32[]{:S(2)}) copy-start(f32[8,256,256]{1,2,0:T(8,128)} %get-tuple-element.34) | copy-start | bytes 6291460
  42.9 1.5 copy-start.5
  43.5 1.0 copy-start.2
  45.5 6.3 %copy-start.3 = (bf16[8,256,256]{1,2,0:T(8,128)(2,1)S(1)}, bf16[8,256,256]{1,2,0:T(8,128)(2,1)}, u32[]{:S(2)}) copy-start(bf16[8,256,256]{1,2,0:T(8,128)(2,1)} %copy-done.2) | copy-start | bytes 3145732
  46.4 7.8 %copy-start.9 = (bf16[1,128,8,128]{3,1,2,0:T(8,128)(2,1)S(1)}, bf16[1,128,8,128]{3,1,2,0:T(8,128)(2,1)}, u32[]{:S(2)}) copy-start(bf16[1,128,8,128]{3,1,2,0:T(8,128)(2,1)} %copy.106) | copy-start | bytes 786436
  54.1 3.3 %copy-start.13 = (bf16[1,128,8,128]{3,1,2,0:T(8,128)(2,1)S(1)}, bf16[1,128,8,128]{3,1,2,0:T(8,128)(2,1)}, u32[]{:S(2)}) copy-start(bf16[1,128,8,128]{3,1,2,0:T(8,128)(2,1)} %copy.108) | copy-start | bytes 786436
  54.1 3.3 %copy-start.14 = (bf16[1,128,8,128]{3,1,2,0:T(8,128)(2,1)S(1)}, bf16[1,128,8,128]{3,1,2,0:T(8,128)(2,1)}, u32[]{:S(2)}) copy-start(bf16[1,128,8,128]{3,1,2,0:T(8,128)(2,1)} %copy.110) | copy-start | bytes 786436
  57.4 2.5 %copy-start.18 = (f32[8,256,256]{1,2,0:T(8,128)S(1)}, f32[8,256,256]{1,2,0:T(8,128)}, u32[]{:S(2)}) copy-start(f32[8,256,256]{1,2,0:T(8,128)} %get-tuple-element.32) | copy-start | bytes 6291460
  59.9 1.5 copy-start.10
  65.2 13.0 %collective-permute-start.5 = (bf16[1,128,8,128]{1,3,2,0:T(8,128)(2,1)}, bf16[1,128,8,128]{1,3,2,0:T(8,128)(2,1)}, u32[]{:S(2)}, u32[]{:S(2)}) collective-permute-start(bf16[1,128,8,128]{1,3,2,0:T(8,128)(2,1)} %get-tuple-element.27), channel_id=1, source_target_pairs={{0,2},{2,4},{4,6},{6,8},{8,10},{10,12},{12,14},{14,16},{16,18},{18... | collective-permute-start | bytes 786440 | tf_op jit(solution)/shard_map/ppermute | solution.py:17
  65.2 11.5 %copy-start.8 = (bf16[1,256,8,128]{1,3,2,0:T(8,128)(2,1)S(1)}, bf16[1,256,8,128]{1,3,2,0:T(8,128)(2,1)}, u32[]{:S(2)}) copy-start(bf16[1,256,8,128]{1,3,2,0:T(8,128)(2,1)} %fusion.18) | copy-start | bytes 1572868
  65.2 11.5 %collective-permute-start.4 = (bf16[1,128,8,128]{1,3,2,0:T(8,128)(2,1)S(1)}, bf16[1,128,8,128]{1,3,2,0:T(8,128)(2,1)S(1)}, u32[]{:S(2)}, u32[]{:S(2)}) collective-permute-start(bf16[1,128,8,128]{1,3,2,0:T(8,128)(2,1)S(1)} %get-tuple-element.29), channel_id=1, source_target_pairs={{0,2},{2,4},{4,6},{6,8},{8,10},{10,12},{12,14},{14,16},{16,18},{18... | collective-permute-start | bytes 786440 | tf_op jit(solution)/shard_map/ppermute | solution.py:17
  69.2 13.5 %collective-permute-start.6 = (bf16[1,128,8,128]{1,3,2,0:T(8,128)(2,1)}, bf16[1,128,8,128]{1,3,2,0:T(8,128)(2,1)}, u32[]{:S(2)}, u32[]{:S(2)}) collective-permute-start(bf16[1,128,8,128]{1,3,2,0:T(8,128)(2,1)} %get-tuple-element.25), channel_id=1, source_target_pairs={{0,2},{2,4},{4,6},{6,8},{8,10},{10,12},{12,14},{14,16},{16,18},{18... | collective-permute-start | bytes 786440 | tf_op jit(solution)/shard_map/ppermute | solution.py:17
  80.5 2.3 copy-start.11
  85.0 2.3 copy-start.15
  87.3 4.5 %copy-start.16 = (bf16[3,8,2048]{2,1,0:T(8,128)(2,1)S(1)}, bf16[3,8,2048]{2,1,0:T(8,128)(2,1)}, u32[]{:S(2)}) copy-start(bf16[3,8,2048]{2,1,0:T(8,128)(2,1)} %param.13) | copy-start | bytes 294916
  97.7 2.4 %copy-start.1 = (bf16[1,256,16,128]{1,3,2,0:T(8,128)(2,1)S(1)}, bf16[1,256,16,128]{1,3,2,0:T(8,128)(2,1)}, u32[]{:S(2)}) copy-start(bf16[1,256,16,128]{1,3,2,0:T(8,128)(2,1)} %maximum_maximum_fusion.2) | copy-start | bytes 3145732
Sparse Core Ops, SparseCore 0:
  96.4 124.8 all-reduce.2
where the time goes:
time: 232 us
  waiting for transfers between devices  127 us (55%)
  local copies, waits for them, and re-layouts  42.2 us (18%)
  matrix products  31.4 us (14%)
  between operations  14.2 us (6%)
  starting transfers between devices  8.49 us (4%)
  other arithmetic  7.93 us (3%)
    psum x1, waiting for transfers between devices, shards(): down_sum, up_sum = lax.psum((down_sum, up_sum), ('seq', 'dp'))  120 us
    unnamed x54, local copies, waits for them, and re-layouts  28.6 us
    ppermute x7, starting transfers between devices, shifted_2(): lax.ppermute(shard, axis, [(i, (i + by) % peers) for i in range(peers)])  8.46 us
    ppermute x7, waiting for transfers between devices, shifted_2(): lax.ppermute(shard, axis, [(i, (i + by) % peers) for i in range(peers)])  7.43 us
    sub x2, matrix products, attend_back(): raised = jnp.exp(scores - highest)  6.65 us
    another operation x3, local copies, waits for them, and re-layouts, shards(): stacked_gradients = jnp.stack(grads).reshape(3, batch * rows, width)  6.03 us
  transfers between devices with their start and end apart: 8, of which 2 were waited for; matrix products, arithmetic and copies ran while one was open for 22% of the time, Pallas kernels for 0%

commit v1 on v0

v1 whole, which is shorter than its diff:
```python
import functools
import math

import jax
import jax.numpy as jnp
from jax import lax
from jax.experimental import pallas as pl
from jax.experimental.pallas import tpu as pltpu
from jax.sharding import PartitionSpec as P

HEAD_FEATURES = 128
ADAPTER_SCALE = 2.0
PLANE_SEQ = 4
F32 = jnp.float32
BF16 = jnp.bfloat16
MESH = pl.DeviceIdType.MESH


def dot(a, b, dims):
    return lax.dot_general(a, b, (dims, ((), ())), preferred_element_type=F32)


def attend_back(query, key, value, gradient, offset):
    scale = 1.0 / math.sqrt(HEAD_FEATURES)
    scores = dot(key, query, ((1,), (1,)))
    shape = scores.shape
    keep = lax.broadcasted_iota(jnp.int32, shape, 0) <= (
        lax.broadcasted_iota(jnp.int32, shape, 1) + offset
    )
    scores = jnp.where(keep, scores, -jnp.inf)
    highest = jnp.max(scores, axis=0, keepdims=True)
    raised = jnp.exp2((scores - highest) * (scale * math.log2(math.e)))
    weights = raised * (1.0 / jnp.sum(raised, axis=0, keepdims=True))
    weights_low = weights.astype(BF16)
    grad_weights = dot(value, gradient, ((1,), (1,)))
    row_dots = jnp.sum(weights_low.astype(F32) * grad_weights, axis=0, keepdims=True)
    grad_scores = (weights * (grad_weights - row_dots)).astype(BF16)
    grad_value = dot(weights_low, gradient, ((1,), (0,)))
    grad_key = dot(grad_scores, query, ((1,), (0,))) * scale
    grad_query = dot(grad_scores, key, ((0,), (0,))) * scale
    return grad_query, grad_key, grad_value


def kernel(
    n_seq, n_dp, tok, q, k, v, g, down_w, up_w, gq, gk, gv, gd, gu,
    kv_in, ret_out, ret_in, part, rs_out, rs_in, zbuf, gbuf,
    kv_send, kv_recv, ret_send, ret_recv, rs_send, rs_recv, z_send, z_recv, ag_send, ag_recv,
):
    rows, width = q.shape[1:]
    model_width = tok.shape[2]
    half, half_width = rows // 2, width // 2
    heads = half_width // HEAD_FEATURES
    seq, dp = lax.axis_index("seq"), lax.axis_index("dp")
    right, left = lax.rem(seq + 1, n_seq), lax.rem(seq + n_seq - 1, n_seq)
    n_plane, n_z = n_dp * PLANE_SEQ, n_seq // PLANE_SEQ
    mine, zone = dp * PLANE_SEQ + lax.rem(seq, PLANE_SEQ), seq // PLANE_SEQ

    def plane_id(j):
        c = lax.rem(mine + j, n_plane)
        return c, {"seq": zone * PLANE_SEQ + lax.rem(c, PLANE_SEQ), "dp": c // PLANE_SEQ}

    def zone_id(j):
        z = lax.rem(zone + j, n_z)
        return z, {"seq": z * PLANE_SEQ + lax.rem(seq, PLANE_SEQ), "dp": dp}

    def remote(src, dst, send, recv, target):
        return pltpu.make_async_remote_copy(
            src_ref=src, dst_ref=dst, send_sem=send, recv_sem=recv,
            device_id=target, device_id_type=MESH,
        )

    barrier = pltpu.get_barrier_semaphore()
    targets = [{"seq": left, "dp": dp}, {"seq": right, "dp": dp}]
    targets += [plane_id(j)[1] for j in range(1, n_plane)]
    targets += [zone_id(j)[1] for j in range(1, n_z)]
    for target in targets:
        pl.semaphore_signal(barrier, inc=1, device_id=target, device_id_type=MESH)
    pl.semaphore_wait(barrier, len(targets))

    upper, lower = pl.ds(half, half), pl.ds(0, half)
    shifted = pl.ds(half_width, half_width)
    kv_copies = [
        remote(
            ref.at[0, upper, shifted], kv_in.at[i], kv_send.at[i], kv_recv.at[i],
            {"seq": right, "dp": dp},
        )
        for i, ref in enumerate((k, v))
    ]
    for copy in kv_copies:
        copy.start()

    def cols(h):
        return pl.ds(pl.multiple_of(h * HEAD_FEATURES, HEAD_FEATURES), HEAD_FEATURES)

    @pl.loop(0, heads, unroll=2)
    def _(h):
        c = cols(h)
        dq, dk, dv = attend_back(q[0, :, c], k[0, :, c], v[0, :, c], g[0, :, c], 0)
        gq[0, :, c] = dq.astype(BF16)
        gk[0, :, c] = dk.astype(BF16)
        gv[0, :, c] = dv.astype(BF16)

    @pl.loop(0, heads, unroll=4)
    def _(h):
        c, s = cols(h + heads), cols(h)
        dq, dk, dv = attend_back(
            q[0, upper, c], k[0, upper, c], v[0, upper, c], g[0, upper, c], 0
        )
        gq[0, upper, c] = dq.astype(BF16)
        part[0, :, s] = dk
        part[1, :, s] = dv

    for copy in kv_copies:
        copy.wait_recv()
    ret_copies = []
    chunks = ret_send.shape[0] // 2
    per = heads // chunks
    for chunk in range(chunks):
        @pl.loop(chunk * per, (chunk + 1) * per, unroll=2)
        def _(h):
            c, s = cols(h + heads), cols(h)
            keys = jnp.concatenate([kv_in[0, :, s], k[0, lower, c]], axis=0)
            values = jnp.concatenate([kv_in[1, :, s], v[0, lower, c]], axis=0)
            dq, dk, dv = attend_back(q[0, lower, c], keys, values, g[0, lower, c], half)
            gq[0, lower, c] = dq.astype(BF16)
            gk[0, lower, c] = dk[half:].astype(BF16)
            gv[0, lower, c] = dv[half:].astype(BF16)
            ret_out[0, :, s] = dk[:half].astype(BF16)
            ret_out[1, :, s] = dv[:half].astype(BF16)

        span = pl.ds(chunk * per * HEAD_FEATURES, per * HEAD_FEATURES)
        for i in range(2):
            at = chunk * 2 + i
            copy = remote(
                ret_out.at[i, :, span], ret_in.at[i, :, span], ret_send.at[at], ret_recv.at[at],
                {"seq": left, "dp": dp},
            )
            copy.start()
            ret_copies.append(copy)

    down_all = jnp.concatenate([down_w[p].astype(F32) for p in range(3)], axis=0).astype(BF16)
    projected = dot(down_all, tok[0], ((1,), (1,)))
    ranks = down_w.shape[1]
    returned, ups = [], []
    for p, ref in enumerate((gq, gk, gv)):
        if p == 1:
            for copy in ret_copies:
                copy.wait_recv()
            gk[0, upper, shifted] = (part[0] + ret_in[0].astype(F32)).astype(BF16)
            gv[0, upper, shifted] = (part[1] + ret_in[1].astype(F32)).astype(BF16)
        grad = ref[0]
        returned.append(dot(up_w[p], grad, ((1,), (1,))))
        ups.append(dot(projected[p * ranks:(p + 1) * ranks].astype(BF16), grad, ((1,), (0,))))
    downs = dot(jnp.concatenate(returned, axis=0).astype(BF16), tok[0], ((1,), (0,)))
    ups = jnp.concatenate(ups, axis=0)

    wd, wu = model_width // n_plane, width // n_plane
    wide = (wd + wu) // 2
    for c in range(n_plane):
        rs_out[c] = jnp.concatenate(
            [
                downs[:, c * wd:c * wd + wide],
                jnp.concatenate(
                    [downs[:, c * wd + wide:(c + 1) * wd], ups[:, c * wu:(c + 1) * wu]], axis=1
                ),
            ],
            axis=0,
        ).astype(BF16)
    copies = []
    for j in range(1, n_plane):
        c, target = plane_id(j)
        copy = remote(rs_out.at[c], rs_in.at[mine], rs_send.at[j], rs_recv.at[j], target)
        copy.start()
        copies.append(copy)
    total = rs_out[mine].astype(F32)
    for j in range(1, n_plane):
        c = lax.rem(mine + n_plane - j, n_plane)
        remote(rs_out.at[c], rs_in.at[c], rs_send.at[j], rs_recv.at[j], plane_id(j)[1]).wait_recv()
        total = total + rs_in[c].astype(F32)
    zbuf[zone] = total.astype(BF16)
    for j in range(1, n_z):
        _, target = zone_id(j)
        copy = remote(zbuf.at[zone], zbuf.at[zone], z_send.at[j], z_recv.at[j], target)
        copy.start()
        copies.append(copy)
    for j in range(1, n_z):
        z = lax.rem(zone + n_z - j, n_z)
        remote(zbuf.at[z], zbuf.at[z], z_send.at[j], z_recv.at[j], zone_id(j)[1]).wait_recv()
    total = zbuf[0].astype(F32)
    for z in range(1, n_z):
        total = total + zbuf[z].astype(F32)
    factor = ADAPTER_SCALE / math.sqrt(rows * n_seq * n_dp)
    gbuf[mine] = (total * factor).astype(BF16)
    for j in range(1, n_plane):
        _, target = plane_id(j)
        copy = remote(gbuf.at[mine], gbuf.at[mine], ag_send.at[j], ag_recv.at[j], target)
        copy.start()
        copies.append(copy)
    for j in range(1, n_plane):
        c = lax.rem(mine + n_plane - j, n_plane)
        remote(gbuf.at[c], gbuf.at[c], ag_send.at[j], ag_recv.at[j], plane_id(j)[1]).wait_recv()
    for c in range(n_plane):
        both = gbuf[c].astype(F32)
        n = both.shape[0] // 2
        down = jnp.concatenate([both[:n], both[n:, :wd - wide]], axis=1)
        up = both[n:, wd - wide:]
        for p in range(3):
            gd[p, :, c * wd:(c + 1) * wd] = down[p * ranks:(p + 1) * ranks]
            gu[p, :, c * wu:(c + 1) * wu] = up[p * ranks:(p + 1) * ranks]
    for copy in kv_copies + ret_copies + copies:
        copy.wait_send()


def shards(n_seq, n_dp, tokens, query, key, value, gradient, down_w, up_w):
    _, rows, width = query.shape
    half, half_width = rows // 2, width // 2
    projections, ranks, model_width = down_w.shape
    n_plane, n_z = n_dp * PLANE_SEQ, n_seq // PLANE_SEQ
    piece = (2 * projections * ranks, (model_width + width) // n_plane // 2)
    dma = pltpu.SemaphoreType.DMA
    vmem = pl.BlockSpec(memory_space=pltpu.VMEM)
    return pl.pallas_call(
        functools.partial(kernel, n_seq, n_dp),
        out_shape=[jax.ShapeDtypeStruct(query.shape, BF16)] * 3
        + [jax.ShapeDtypeStruct(down_w.shape, F32), jax.ShapeDtypeStruct(up_w.shape, F32)],
        in_specs=[vmem] * 7,
        out_specs=[vmem] * 5,
        scratch_shapes=[
            pltpu.VMEM((2, half, half_width), BF16),
            pltpu.VMEM((2, half, half_width), BF16),
            pltpu.VMEM((2, half, half_width), BF16),
            pltpu.VMEM((2, half, half_width), F32),
            pltpu.VMEM((n_plane,) + piece, BF16),
            pltpu.VMEM((n_plane,) + piece, BF16),
            pltpu.VMEM((n_z,) + piece, BF16),
            pltpu.VMEM((n_plane,) + piece, BF16),
            dma((2,)), dma((2,)), dma((4,)), dma((4,)),
            dma((n_plane,)), dma((n_plane,)), dma((n_z,)), dma((n_z,)),
            dma((n_plane,)), dma((n_plane,)),
        ],
        compiler_params=pltpu.CompilerParams(
            collective_id=0, has_side_effects=True, vmem_limit_bytes=56 * 1024 * 1024
        ),
    )(tokens, query, key, value, gradient, down_w, up_w)


def solution(mesh):
    split = P("dp", "seq", None)
    return jax.shard_map(
        functools.partial(shards, mesh.shape["seq"], mesh.shape["dp"]),
        mesh=mesh,
        in_specs=(split,) * 5 + (P(), P()),
        out_specs=(split,) * 3 + (P(), P()),
        check_vma=False,
    )
```

time: 232 us -> 50.5 us (0.22)
  waiting for transfers between devices: 127 us -> 0 us
  Pallas kernels: 0 us -> 43.8 us
  local copies, waits for them, and re-layouts: 42.2 us -> 5.83 us
  matrix products: 31.4 us -> 0 us
  between operations: 14.2 us -> 0.66 us
  starting transfers between devices: 8.49 us -> 0 us
  other arithmetic: 7.93 us -> 0 us
    psum x1 -> x0, waiting for transfers between devices: 120 us -> none  [shards(): down_sum, up_sum = lax.psum((down_sum, up_sum), ('seq', 'dp'))]
    pallas_call x0 -> x1, Pallas kernels: none -> 43.8 us  [shards(): pl.pallas_call(functools.partial(kernel, n_seq, n_dp), out_shape=[jax.Sha...]
    dot_general x12 -> x0, matrix products: 24.7 us -> none  [the longest x1 4.52 us: shards(): jnp.einsum('pnr,pnh->prh', down_projected, stacked_gradients, preferred_e...]
    unnamed x54 -> x13, local copies, waits for them, and re-layouts: 28.6 us -> 5.83 us
    ppermute x7 -> x0, starting transfers between devices: 8.46 us -> none  [shifted_2(): lax.ppermute(shard, axis, [(i, (i + by) % peers) for i in range(peers)])]
    slice x8 -> x0, local copies, waits for them, and re-layouts: 7.58 us -> none  [the longest x3 1.89 us: shards(): lower = [part[:, half_rows:].astype(jnp.bfloat16) for part in group]]
    ppermute x7 -> x0, waiting for transfers between devices: 7.43 us -> none  [shifted_2(): lax.ppermute(shard, axis, [(i, (i + by) % peers) for i in range(peers)])]
    sub x2 -> x0, matrix products: 6.65 us -> none  [attend_back(): raised = jnp.exp(scores - highest)]
  transfers between devices with their start and end apart: 8 -> 0, of which waited for: 2 -> 0; matrix products, arithmetic and copies ran while one was open for 22% -> 0% of each run, Pallas kernels for 0% -> 0%
where the time goes in v1:
time: 50.5 us; the launch traced here: 50.3 us
  Pallas kernels  43.8 us (87%)
  local copies, waits for them, and re-layouts  5.83 us (12%)
  between operations  0.66 us (1%)
    pallas_call x1, Pallas kernels, shards(): pl.pallas_call(functools.partial(kernel, n_seq, n_dp), out_shape=[jax.Sha...  43.8 us
    unnamed x13, local copies, waits for them, and re-layouts  5.83 us

profile of v1, /device:TPU:0, one launch (start us, length us, event | category | flops | bytes accessed | tf_op | source)
XLA Modules:
  0.0 50.3 jit_solution(5035406224464575334)
XLA Ops:
  0.6 43.8 %shard_map.110 = (bf16[1,256,2048]{2,1,0:T(8,128)(2,1)}, bf16[1,256,2048]{2,1,0:T(8,128)(2,1)}, bf16[1,256,2048]{2,1,0:T(8,128)(2,1)}, f32[3,8,4096]{2,1,0:T(8,128)}, f32[3,8,2048]{2,1,0:T(8,128)}) custom-call(bf16[1,256,4096]{2,1,0:T(8,128)(2,1)} %tok.1, bf16[1,256,2048]{2,1,0:T(8,128)(2,1)} %q.1, bf16[1,256,2048]{2,1,0:T(8,128)(2,1)} %k.1, ...), custom_call_target="tpu_custom_call" | custom-call | tf_op jit(solution)/shard_map/pallas_call | solution.py:222
  44.5 0.0 copy-start.1
  44.5 0.0 copy-start
  44.5 2.5 %copy.17 = bf16[1,256,2048]{2,1,0:T(8,128)(2,1)} copy(bf16[1,256,2048]{2,1,0:T(8,128)(2,1)} %get-tuple-element.10) | data formatting | bytes 2097152
  46.9 0.0 copy-done.1
  46.9 0.0 copy-start.2
  46.9 0.0 copy-start.3
  46.9 1.0 %copy.18 = bf16[1,256,2048]{2,1,0:T(8,128)(2,1)} copy(bf16[1,256,2048]{2,1,0:T(8,128)(2,1)S(1)} %copy-done.1) | data formatting | bytes 2097152
  47.9 0.0 copy-done
  47.9 1.0 %copy.19 = bf16[1,256,2048]{2,1,0:T(8,128)(2,1)} copy(bf16[1,256,2048]{2,1,0:T(8,128)(2,1)S(1)} %copy-done) | data formatting | bytes 2097152
  48.9 0.0 copy-done.2
  48.9 0.7 %copy.20 = f32[3,8,4096]{2,1,0:T(8,128)} copy(f32[3,8,4096]{2,1,0:T(8,128)S(1)} %copy-done.2) | data formatting | bytes 786432
  49.6 0.0 copy-done.3
  49.6 0.7 %copy.21 = f32[3,8,2048]{2,1,0:T(8,128)} copy(f32[3,8,2048]{2,1,0:T(8,128)S(1)} %copy-done.3) | data formatting | bytes 393216
Async XLA Ops:
  44.5 2.5 %copy-start.1 = (bf16[1,256,2048]{2,1,0:T(8,128)(2,1)S(1)}, bf16[1,256,2048]{2,1,0:T(8,128)(2,1)}, u32[]{:S(2)}) copy-start(bf16[1,256,2048]{2,1,0:T(8,128)(2,1)} %get-tuple-element.11) | copy-start | bytes 3145732
  44.5 3.4 %copy-start = (bf16[1,256,2048]{2,1,0:T(8,128)(2,1)S(1)}, bf16[1,256,2048]{2,1,0:T(8,128)(2,1)}, u32[]{:S(2)}) copy-start(bf16[1,256,2048]{2,1,0:T(8,128)(2,1)} %get-tuple-element.12) | copy-start | bytes 3145732
  46.9 1.9 %copy-start.2 = (f32[3,8,4096]{2,1,0:T(8,128)S(1)}, f32[3,8,4096]{2,1,0:T(8,128)}, u32[]{:S(2)}) copy-start(f32[3,8,4096]{2,1,0:T(8,128)} %get-tuple-element.13) | copy-start | bytes 1179652
  46.9 2.7 %copy-start.3 = (f32[3,8,2048]{2,1,0:T(8,128)S(1)}, f32[3,8,2048]{2,1,0:T(8,128)}, u32[]{:S(2)}) copy-start(f32[3,8,2048]{2,1,0:T(8,128)} %get-tuple-element.14) | copy-start | bytes 589828

commit v2 on v1

--- a/solution.py
+++ b/solution.py
@@ -42,7 +42,7 @@
 
 
 def kernel(
-    n_seq, n_dp, tok, q, k, v, g, down_w, up_w, gq, gk, gv, gd, gu,
+    n_seq, n_dp, tok, q, k, v, g, down_w, up_w, gq, gk, gv, gbuf_out,
     kv_in, ret_out, ret_in, part, rs_out, rs_in, zbuf, gbuf,
     kv_send, kv_recv, ret_send, ret_recv, rs_send, rs_recv, z_send, z_recv, ag_send, ag_recv,
 ):
@@ -199,16 +199,36 @@
     for j in range(1, n_plane):
         c = lax.rem(mine + n_plane - j, n_plane)
         remote(gbuf.at[c], gbuf.at[c], ag_send.at[j], ag_recv.at[j], plane_id(j)[1]).wait_recv()
-    for c in range(n_plane):
-        both = gbuf[c].astype(F32)
-        n = both.shape[0] // 2
-        down = jnp.concatenate([both[:n], both[n:, :wd - wide]], axis=1)
-        up = both[n:, wd - wide:]
-        for p in range(3):
-            gd[p, :, c * wd:(c + 1) * wd] = down[p * ranks:(p + 1) * ranks]
-            gu[p, :, c * wu:(c + 1) * wu] = up[p * ranks:(p + 1) * ranks]
+    gbuf_out[...] = gbuf[...]
     for copy in kv_copies + ret_copies + copies:
         copy.wait_send()
+
+
+def finish(n_plane, gq_in, gk_in, gv_in, sums, gq, gk, gv, gd, gu, down, up, sems):
+    copies = [
+        pltpu.make_async_copy(src, dst, sems.at[i])
+        for i, (src, dst) in enumerate(((gq_in, gq), (gk_in, gk), (gv_in, gv)))
+    ]
+    for copy in copies:
+        copy.start()
+    projections, ranks, model_width = down.shape
+    wd, wu = model_width // n_plane, up.shape[2] // n_plane
+    wide = (wd + wu) // 2
+    n = projections * ranks
+    for c in range(n_plane):
+        both = sums[c].astype(F32)
+        for p in range(projections):
+            at = p * ranks
+            down[p, :, c * wd:c * wd + wide] = both[at:at + ranks]
+            down[p, :, c * wd + wide:(c + 1) * wd] = both[n + at:n + at + ranks, :wd - wide]
+            up[p, :, c * wu:(c + 1) * wu] = both[n + at:n + at + ranks, wd - wide:]
+    last = [
+        pltpu.make_async_copy(down, gd, sems.at[3]), pltpu.make_async_copy(up, gu, sems.at[4])
+    ]
+    for copy in last:
+        copy.start()
+    for copy in copies + last:
+        copy.wait()
 
 
 def shards(n_seq, n_dp, tokens, query, key, value, gradient, down_w, up_w):
@@ -219,12 +239,12 @@
     piece = (2 * projections * ranks, (model_width + width) // n_plane // 2)
     dma = pltpu.SemaphoreType.DMA
     vmem = pl.BlockSpec(memory_space=pltpu.VMEM)
-    return pl.pallas_call(
+    *grads, sums = pl.pallas_call(
         functools.partial(kernel, n_seq, n_dp),
         out_shape=[jax.ShapeDtypeStruct(query.shape, BF16)] * 3
-        + [jax.ShapeDtypeStruct(down_w.shape, F32), jax.ShapeDtypeStruct(up_w.shape, F32)],
+        + [jax.ShapeDtypeStruct((n_plane,) + piece, BF16)],
         in_specs=[vmem] * 7,
-        out_specs=[vmem] * 5,
+        out_specs=[vmem] * 4,
         scratch_shapes=[
             pltpu.VMEM((2, half, half_width), BF16),
             pltpu.VMEM((2, half, half_width), BF16),
@@ -239,9 +259,21 @@
             dma((n_plane,)), dma((n_plane,)),
         ],
         compiler_params=pltpu.CompilerParams(
-            collective_id=0, has_side_effects=True, vmem_limit_bytes=56 * 1024 * 1024
+            collective_id=0, has_side_effects=True, vmem_limit_bytes=36 * 1024 * 1024
         ),
     )(tokens, query, key, value, gradient, down_w, up_w)
+    anywhere = pl.BlockSpec(memory_space=pl.ANY)
+    return pl.pallas_call(
+        functools.partial(finish, n_plane),
+        out_shape=[jax.ShapeDtypeStruct(query.shape, BF16)] * 3
+        + [jax.ShapeDtypeStruct(down_w.shape, F32), jax.ShapeDtypeStruct(up_w.shape, F32)],
+        in_specs=[anywhere] * 3 + [vmem],
+        out_specs=[anywhere] * 5,
+        scratch_shapes=[
+            pltpu.VMEM(down_w.shape, F32), pltpu.VMEM(up_w.shape, F32), dma((5,)),
+        ],
+        compiler_params=pltpu.CompilerParams(vmem_limit_bytes=8 * 1024 * 1024),
+    )(*grads, sums)
 
 
 def solution(mesh):

time: 50.5 us -> 50.3 us (level)
  Pallas kernels: 43.8 us -> 41 us
  local copies, waits for them, and re-layouts: 5.83 us -> 8.3 us
    pallas_call x1, Pallas kernels: 43.8 us -> 39.1 us  [shards(): pl.pallas_call(functools.partial(kernel, n_seq, n_dp), out_shape=[jax.Sha...]
    unnamed x13 -> x14, local copies, waits for them, and re-layouts: 5.83 us -> 8.3 us
    pallas_call x0 -> x1, Pallas kernels: none -> 1.89 us  [shards(): pl.pallas_call(functools.partial(finish, n_plane), out_shape=[jax.ShapeDt...]
where the time goes in v2:
time: 50.3 us; the launch traced here: 49.9 us
  Pallas kernels  41 us (82%)
  local copies, waits for them, and re-layouts  8.3 us (17%)
  between operations  0.66 us (1%)
    pallas_call x1, Pallas kernels, shards(): pl.pallas_call(functools.partial(kernel, n_seq, n_dp), out_shape=[jax.Sha...  39.1 us
    unnamed x14, local copies, waits for them, and re-layouts  8.3 us
    pallas_call x1, Pallas kernels, shards(): pl.pallas_call(functools.partial(finish, n_plane), out_shape=[jax.ShapeDt...  1.89 us

profile of v2, /device:TPU:0, one launch (start us, length us, event | category | flops | bytes accessed | tf_op | source)
XLA Modules:
  0.0 49.9 jit_solution(3367049558924242234)
XLA Ops:
  0.6 0.0 copy-start
  0.6 1.6 %copy-done = bf16[1,256,4096]{2,1,0:T(8,128)(2,1)S(1)} copy-done((bf16[1,256,4096]{2,1,0:T(8,128)(2,1)S(1)}, bf16[1,256,4096]{2,1,0:T(8,128)(2,1)}, u32[]{:S(2)}) %copy-start) | copy-done | bytes 2097176
  2.2 0.0 copy-start.1
  2.2 1.2 %copy-done.1 = bf16[1,256,2048]{2,1,0:T(8,128)(2,1)S(1)} copy-done((bf16[1,256,2048]{2,1,0:T(8,128)(2,1)S(1)}, bf16[1,256,2048]{2,1,0:T(8,128)(2,1)}, u32[]{:S(2)}) %copy-start.1) | copy-done | bytes 1048600
  3.5 0.0 copy-start.2
  3.5 1.2 %copy-done.2 = bf16[1,256,2048]{2,1,0:T(8,128)(2,1)S(1)} copy-done((bf16[1,256,2048]{2,1,0:T(8,128)(2,1)S(1)}, bf16[1,256,2048]{2,1,0:T(8,128)(2,1)}, u32[]{:S(2)}) %copy-start.2) | copy-done | bytes 1048600
  4.7 0.0 copy-start.3
  4.7 1.2 %copy-done.3 = bf16[1,256,2048]{2,1,0:T(8,128)(2,1)S(1)} copy-done((bf16[1,256,2048]{2,1,0:T(8,128)(2,1)S(1)}, bf16[1,256,2048]{2,1,0:T(8,128)(2,1)}, u32[]{:S(2)}) %copy-start.3) | copy-done | bytes 1048600
  5.9 0.0 copy-start.4
  5.9 1.2 %copy-done.4 = bf16[1,256,2048]{2,1,0:T(8,128)(2,1)S(1)} copy-done((bf16[1,256,2048]{2,1,0:T(8,128)(2,1)S(1)}, bf16[1,256,2048]{2,1,0:T(8,128)(2,1)}, u32[]{:S(2)}) %copy-start.4) | copy-done | bytes 1048600
  7.1 0.0 copy-start.5
  7.1 0.9 %copy-done.5 = bf16[3,8,4096]{2,1,0:T(8,128)(2,1)S(1)} copy-done((bf16[3,8,4096]{2,1,0:T(8,128)(2,1)S(1)}, bf16[3,8,4096]{2,1,0:T(8,128)(2,1)}, u32[]{:S(2)}) %copy-start.5) | copy-done | bytes 196632
  8.1 0.0 copy-start.6
  8.1 0.9 %copy-done.6 = bf16[3,8,2048]{2,1,0:T(8,128)(2,1)S(1)} copy-done((bf16[3,8,2048]{2,1,0:T(8,128)(2,1)S(1)}, bf16[3,8,2048]{2,1,0:T(8,128)(2,1)}, u32[]{:S(2)}) %copy-start.6) | copy-done | bytes 98328
  8.9 39.1 %shard_map.110 = (bf16[1,256,2048]{2,1,0:T(8,128)(2,1)S(1)}, bf16[1,256,2048]{2,1,0:T(8,128)(2,1)S(1)}, bf16[1,256,2048]{2,1,0:T(8,128)(2,1)S(1)}, bf16[8,48,384]{2,1,0:T(8,128)(2,1)S(1)}) custom-call(bf16[1,256,4096]{2,1,0:T(8,128)(2,1)S(1)} %copy-done, bf16[1,256,2048]{2,1,0:T(8,128)(2,1)S(1)} %copy-done.1, bf16[1,256,2048]{2,1,0:T(8,128)(2,1)S(1)} %copy-done.2, ...), custom_call_target="tpu_custom_call" | custom-call | tf_op jit(solution)/shard_map/pallas_call | solution.py:242
  48.0 1.9 %shard_map.111 = (bf16[1,256,2048]{2,1,0:T(8,128)(2,1)}, bf16[1,256,2048]{2,1,0:T(8,128)(2,1)}, bf16[1,256,2048]{2,1,0:T(8,128)(2,1)}, f32[3,8,4096]{2,1,0:T(8,128)}, f32[3,8,2048]{2,1,0:T(8,128)}) custom-call(bf16[1,256,2048]{2,1,0:T(8,128)(2,1)S(1)} %get-tuple-element.9.gq_in, bf16[1,256,2048]{2,1,0:T(8,128)(2,1)S(1)} %get-tuple-element.10.gk_in, ...), custom_call_target="tpu_custom_call" | custom-call | tf_op jit(solution)/shard_map/pallas_call | solution.py:266
Async XLA Ops:
  0.6 1.6 %copy-start = (bf16[1,256,4096]{2,1,0:T(8,128)(2,1)S(1)}, bf16[1,256,4096]{2,1,0:T(8,128)(2,1)}, u32[]{:S(2)}) copy-start(bf16[1,256,4096]{2,1,0:T(8,128)(2,1)} %tok.1) | copy-start | bytes 6291460
  2.2 1.2 %copy-start.1 = (bf16[1,256,2048]{2,1,0:T(8,128)(2,1)S(1)}, bf16[1,256,2048]{2,1,0:T(8,128)(2,1)}, u32[]{:S(2)}) copy-start(bf16[1,256,2048]{2,1,0:T(8,128)(2,1)} %q.1) | copy-start | bytes 3145732
  3.5 1.2 %copy-start.2 = (bf16[1,256,2048]{2,1,0:T(8,128)(2,1)S(1)}, bf16[1,256,2048]{2,1,0:T(8,128)(2,1)}, u32[]{:S(2)}) copy-start(bf16[1,256,2048]{2,1,0:T(8,128)(2,1)} %k.1) | copy-start | bytes 3145732
  4.7 1.2 %copy-start.3 = (bf16[1,256,2048]{2,1,0:T(8,128)(2,1)S(1)}, bf16[1,256,2048]{2,1,0:T(8,128)(2,1)}, u32[]{:S(2)}) copy-start(bf16[1,256,2048]{2,1,0:T(8,128)(2,1)} %v.1) | copy-start | bytes 3145732
  5.9 1.2 %copy-start.4 = (bf16[1,256,2048]{2,1,0:T(8,128)(2,1)S(1)}, bf16[1,256,2048]{2,1,0:T(8,128)(2,1)}, u32[]{:S(2)}) copy-start(bf16[1,256,2048]{2,1,0:T(8,128)(2,1)} %g.1) | copy-start | bytes 3145732
  7.1 0.9 %copy-start.5 = (bf16[3,8,4096]{2,1,0:T(8,128)(2,1)S(1)}, bf16[3,8,4096]{2,1,0:T(8,128)(2,1)}, u32[]{:S(2)}) copy-start(bf16[3,8,4096]{2,1,0:T(8,128)(2,1)} %down_w.1) | copy-start | bytes 589828
  8.1 0.9 %copy-start.6 = (bf16[3,8,2048]{2,1,0:T(8,128)(2,1)S(1)}, bf16[3,8,2048]{2,1,0:T(8,128)(2,1)}, u32[]{:S(2)}) copy-start(bf16[3,8,2048]{2,1,0:T(8,128)(2,1)} %up_w.1) | copy-start | bytes 294916

commit v3 on v2

v3 whole, which is shorter than its diff:
```python
import functools
import math

import jax
import jax.numpy as jnp
from jax import lax
from jax.experimental import pallas as pl
from jax.experimental.pallas import tpu as pltpu
from jax.sharding import PartitionSpec as P

HEAD_FEATURES = 128
ADAPTER_SCALE = 2.0
PLANE_SEQ = 4
F32 = jnp.float32
BF16 = jnp.bfloat16
MESH = pl.DeviceIdType.MESH


def dot(a, b, dims):
    return lax.dot_general(a, b, (dims, ((), ())), preferred_element_type=F32)


def attend_back(query, key, value, gradient, offset):
    scale = 1.0 / math.sqrt(HEAD_FEATURES)
    scores = dot(key, query, ((1,), (1,)))
    shape = scores.shape
    keep = lax.broadcasted_iota(jnp.int32, shape, 0) <= (
        lax.broadcasted_iota(jnp.int32, shape, 1) + offset
    )
    scores = jnp.where(keep, scores, -jnp.inf)
    highest = jnp.max(scores, axis=0, keepdims=True)
    raised = jnp.exp2((scores - highest) * (scale * math.log2(math.e)))
    weights = raised * (1.0 / jnp.sum(raised, axis=0, keepdims=True))
    weights_low = weights.astype(BF16)
    grad_weights = dot(value, gradient, ((1,), (1,)))
    row_dots = jnp.sum(weights_low.astype(F32) * grad_weights, axis=0, keepdims=True)
    grad_scores = (weights * (grad_weights - row_dots)).astype(BF16)
    grad_value = dot(weights_low, gradient, ((1,), (0,)))
    grad_key = dot(grad_scores, query, ((1,), (0,))) * scale
    grad_query = dot(grad_scores, key, ((0,), (0,))) * scale
    return grad_query, grad_key, grad_value


def kernel(
    n_seq, n_dp, tok_hbm, q_hbm, k_hbm, v_hbm, g_hbm, down_hbm, up_hbm, gq_hbm, gk_hbm, gv_hbm, first_out, last_out,
    gq, gk, gv, tok, q, k, v, g, down_w, up_w, kv_in, ret_out, ret_in, part,
    rs_out0, rs_in0, zbuf0, gbuf0, rs_out1, rs_in1, zbuf1, gbuf1,
    load_sem, store_sem, kv_send, kv_recv, ret_send, ret_recv,
    rs_send, rs_recv, z_send, z_recv, ag_send, ag_recv,
):
    rows, width = q.shape[1:]
    model_width = tok.shape[2]
    half, half_width = rows // 2, width // 2
    heads = half_width // HEAD_FEATURES
    seq, dp = lax.axis_index("seq"), lax.axis_index("dp")
    right, left = lax.rem(seq + 1, n_seq), lax.rem(seq + n_seq - 1, n_seq)
    n_plane, n_z = n_dp * PLANE_SEQ, n_seq // PLANE_SEQ
    mine, zone = dp * PLANE_SEQ + lax.rem(seq, PLANE_SEQ), seq // PLANE_SEQ

    def plane_id(j):
        c = lax.rem(mine + j, n_plane)
        return c, {"seq": zone * PLANE_SEQ + lax.rem(c, PLANE_SEQ), "dp": c // PLANE_SEQ}

    def zone_id(j):
        z = lax.rem(zone + j, n_z)
        return z, {"seq": z * PLANE_SEQ + lax.rem(seq, PLANE_SEQ), "dp": dp}

    def remote(src, dst, send, recv, target):
        return pltpu.make_async_remote_copy(
            src_ref=src, dst_ref=dst, send_sem=send, recv_sem=recv,
            device_id=target, device_id_type=MESH,
        )

    loads = [
        pltpu.make_async_copy(src, dst, load_sem.at[i])
        for i, (src, dst) in enumerate(
            ((q_hbm, q), (k_hbm, k), (v_hbm, v), (g_hbm, g),
             (down_hbm, down_w), (up_hbm, up_w), (tok_hbm, tok))
        )
    ]
    for copy in loads:
        copy.start()
    barrier = pltpu.get_barrier_semaphore()
    targets = [{"seq": left, "dp": dp}, {"seq": right, "dp": dp}]
    targets += [plane_id(j)[1] for j in range(1, n_plane)]
    targets += [zone_id(j)[1] for j in range(1, n_z)]
    for target in targets:
        pl.semaphore_signal(barrier, inc=1, device_id=target, device_id_type=MESH)
    pl.semaphore_wait(barrier, len(targets))

    upper, lower = pl.ds(half, half), pl.ds(0, half)
    shifted = pl.ds(half_width, half_width)
    kv_copies = [
        remote(
            ref.at[0, upper, shifted], kv_in.at[i], kv_send.at[i], kv_recv.at[i],
            {"seq": right, "dp": dp},
        )
        for i, ref in enumerate((k_hbm, v_hbm))
    ]
    for copy in kv_copies:
        copy.start()
    for copy in loads[:4]:
        copy.wait()

    def cols(h):
        return pl.ds(pl.multiple_of(h * HEAD_FEATURES, HEAD_FEATURES), HEAD_FEATURES)

    @pl.loop(0, heads, unroll=2)
    def _(h):
        c = cols(h)
        dq, dk, dv = attend_back(q[0, :, c], k[0, :, c], v[0, :, c], g[0, :, c], 0)
        gq[0, :, c] = dq.astype(BF16)
        gk[0, :, c] = dk.astype(BF16)
        gv[0, :, c] = dv.astype(BF16)

    @pl.loop(0, heads, unroll=4)
    def _(h):
        c, s = cols(h + heads), cols(h)
        dq, dk, dv = attend_back(
            q[0, upper, c], k[0, upper, c], v[0, upper, c], g[0, upper, c], 0
        )
        gq[0, upper, c] = dq.astype(BF16)
        part[0, :, s] = dk
        part[1, :, s] = dv

    for copy in kv_copies:
        copy.wait_recv()
    ret_copies = []
    chunks = ret_send.shape[0] // 2
    per = heads // chunks
    for chunk in range(chunks):
        @pl.loop(chunk * per, (chunk + 1) * per, unroll=2)
        def _(h):
            c, s = cols(h + heads), cols(h)
            keys = jnp.concatenate([kv_in[0, :, s], k[0, lower, c]], axis=0)
            values = jnp.concatenate([kv_in[1, :, s], v[0, lower, c]], axis=0)
            dq, dk, dv = attend_back(q[0, lower, c], keys, values, g[0, lower, c], half)
            gq[0, lower, c] = dq.astype(BF16)
            gk[0, lower, c] = dk[half:].astype(BF16)
            gv[0, lower, c] = dv[half:].astype(BF16)
            ret_out[0, :, s] = dk[:half].astype(BF16)
            ret_out[1, :, s] = dv[:half].astype(BF16)

        span = pl.ds(chunk * per * HEAD_FEATURES, per * HEAD_FEATURES)
        for i in range(2):
            at = chunk * 2 + i
            copy = remote(
                ret_out.at[i, :, span], ret_in.at[i, :, span], ret_send.at[at], ret_recv.at[at],
                {"seq": left, "dp": dp},
            )
            copy.start()
            ret_copies.append(copy)

    for copy in loads[4:]:
        copy.wait()
    ranks = down_w.shape[1]
    wd, wu = model_width // n_plane, width // n_plane
    wide = (wd + wu) // 2
    factor = ADAPTER_SCALE / math.sqrt(rows * n_seq * n_dp)
    buffers = ((rs_out0, rs_in0, zbuf0, gbuf0), (rs_out1, rs_in1, zbuf1, gbuf1))
    copies = []
    stores = [
        pltpu.make_async_copy(src, dst, store_sem.at[i])
        for i, (src, dst) in enumerate(((gq, gq_hbm), (gk, gk_hbm), (gv, gv_hbm)))
    ]
    stores[0].start()

    def scatter(group, downs, ups):
        rs_out, rs_in, _, _ = buffers[group]
        for c in range(n_plane):
            tail = [downs[:, c * wd + wide:(c + 1) * wd], ups[:, c * wu:(c + 1) * wu]]
            rs_out[c] = jnp.concatenate(
                [downs[:, c * wd:c * wd + wide], jnp.concatenate(tail, axis=1)], axis=0
            ).astype(BF16)
        for j in range(1, n_plane):
            c, target = plane_id(j)
            copy = remote(
                rs_out.at[c], rs_in.at[mine], rs_send.at[group, j], rs_recv.at[group, j], target
            )
            copy.start()
            copies.append(copy)

    def exchange(group):
        rs_out, rs_in, zbuf, _ = buffers[group]
        total = rs_out[mine].astype(F32)
        for j in range(1, n_plane):
            c = lax.rem(mine + n_plane - j, n_plane)
            remote(
                rs_out.at[c], rs_in.at[c], rs_send.at[group, j], rs_recv.at[group, j],
                plane_id(j)[1],
            ).wait_recv()
            total = total + rs_in[c].astype(F32)
        zbuf[zone] = total.astype(BF16)
        for j in range(1, n_z):
            copy = remote(
                zbuf.at[zone], zbuf.at[zone], z_send.at[group, j], z_recv.at[group, j],
                zone_id(j)[1],
            )
            copy.start()
            copies.append(copy)

    def gather(group):
        _, _, zbuf, gbuf = buffers[group]
        for j in range(1, n_z):
            z = lax.rem(zone + n_z - j, n_z)
            remote(
                zbuf.at[z], zbuf.at[z], z_send.at[group, j], z_recv.at[group, j], zone_id(j)[1]
            ).wait_recv()
        total = zbuf[0].astype(F32)
        for z in range(1, n_z):
            total = total + zbuf[z].astype(F32)
        gbuf[mine] = (total * factor).astype(BF16)
        for j in range(1, n_plane):
            copy = remote(
                gbuf.at[mine], gbuf.at[mine], ag_send.at[group, j], ag_recv.at[group, j],
                plane_id(j)[1],
            )
            copy.start()
            copies.append(copy)

    def collect(group, out):
        gbuf = buffers[group][3]
        for j in range(1, n_plane):
            c = lax.rem(mine + n_plane - j, n_plane)
            remote(
                gbuf.at[c], gbuf.at[c], ag_send.at[group, j], ag_recv.at[group, j], plane_id(j)[1]
            ).wait_recv()
        out[...] = gbuf[...]

    down_all = jnp.concatenate([down_w[p].astype(F32) for p in range(3)], axis=0).astype(BF16)
    projected = dot(down_all, tok[0], ((1,), (1,)))

    def adapters(parts):
        returned, ups = [], []
        for p, ref in parts:
            grad = ref[0]
            returned.append(dot(up_w[p], grad, ((1,), (1,))))
            mid = projected[p * ranks:(p + 1) * ranks].astype(BF16)
            ups.append(dot(mid, grad, ((1,), (0,))))
        downs = dot(jnp.concatenate(returned, axis=0).astype(BF16), tok[0], ((1,), (0,)))
        return downs, jnp.concatenate(ups, axis=0)

    scatter(0, *adapters(((0, gq),)))
    exchange(0)
    for copy in ret_copies:
        copy.wait_recv()
    gk[0, upper, shifted] = (part[0] + ret_in[0].astype(F32)).astype(BF16)
    gv[0, upper, shifted] = (part[1] + ret_in[1].astype(F32)).astype(BF16)
    for copy in stores[1:]:
        copy.start()
    scatter(1, *adapters(((1, gk), (2, gv))))
    gather(0)
    exchange(1)
    collect(0, first_out)
    gather(1)
    collect(1, last_out)
    for copy in stores:
        copy.wait()
    for copy in kv_copies + ret_copies + copies:
        copy.wait_send()


def finish(n_plane, gq_in, gk_in, gv_in, first, last_two, gq, gk, gv, gd, gu, down, up, sems):
    copies = [
        pltpu.make_async_copy(src, dst, sems.at[i])
        for i, (src, dst) in enumerate(((gq_in, gq), (gk_in, gk), (gv_in, gv)))
    ]
    for copy in copies:
        copy.start()
    projections, ranks, model_width = down.shape
    wd, wu = model_width // n_plane, up.shape[2] // n_plane
    wide = (wd + wu) // 2
    for sums, start, count in ((first, 0, 1), (last_two, 1, projections - 1)):
        n = count * ranks
        for c in range(n_plane):
            both = sums[c].astype(F32)
            for p in range(count):
                top = both[p * ranks:(p + 1) * ranks]
                low = both[n + p * ranks:n + (p + 1) * ranks]
                down[start + p, :, c * wd:c * wd + wide] = top
                down[start + p, :, c * wd + wide:(c + 1) * wd] = low[:, :wd - wide]
                up[start + p, :, c * wu:(c + 1) * wu] = low[:, wd - wide:]
    last = [
        pltpu.make_async_copy(down, gd, sems.at[3]), pltpu.make_async_copy(up, gu, sems.at[4])
    ]
    for copy in last:
        copy.start()
    for copy in copies + last:
        copy.wait()


def shards(n_seq, n_dp, tokens, query, key, value, gradient, down_w, up_w):
    _, rows, width = query.shape
    half, half_width = rows // 2, width // 2
    projections, ranks, model_width = down_w.shape
    n_plane, n_z = n_dp * PLANE_SEQ, n_seq // PLANE_SEQ
    across = (model_width + width) // n_plane // 2
    first, last_two = (2 * ranks, across), (2 * (projections - 1) * ranks, across)
    dma = pltpu.SemaphoreType.DMA
    anywhere = pl.BlockSpec(memory_space=pl.ANY)
    vmem = pl.BlockSpec(memory_space=pltpu.VMEM)
    *grads, first_sums, last_sums = pl.pallas_call(
        functools.partial(kernel, n_seq, n_dp),
        out_shape=[jax.ShapeDtypeStruct(query.shape, BF16)] * 3
        + [jax.ShapeDtypeStruct((n_plane,) + piece, BF16) for piece in (first, last_two)],
        in_specs=[anywhere] * 7,
        out_specs=[anywhere] * 3 + [vmem] * 2,
        scratch_shapes=[
            pltpu.VMEM(ref.shape, BF16)
            for ref in (query, query, query, tokens, query, key, value, gradient, down_w, up_w)
        ]
        + [pltpu.VMEM((2, half, half_width), BF16)] * 3
        + [pltpu.VMEM((2, half, half_width), F32)]
        + [
            pltpu.VMEM((n,) + piece, BF16)
            for piece in (first, last_two)
            for n in (n_plane, n_plane, n_z, n_plane)
        ]
        + [dma((7,)), dma((3,)), dma((2,)), dma((2,)), dma((4,)), dma((4,))]
        + [dma((2, n)) for n in (n_plane, n_plane, n_z, n_z, n_plane, n_plane)],
        compiler_params=pltpu.CompilerParams(
            collective_id=0, has_side_effects=True, vmem_limit_bytes=58 * 1024 * 1024
        ),
    )(tokens, query, key, value, gradient, down_w, up_w)
    return pl.pallas_call(
        functools.partial(finish, n_plane),
        out_shape=[jax.ShapeDtypeStruct(query.shape, BF16)] * 3
        + [jax.ShapeDtypeStruct(down_w.shape, F32), jax.ShapeDtypeStruct(up_w.shape, F32)],
        in_specs=[anywhere] * 3 + [vmem] * 2,
        out_specs=[anywhere] * 5,
        scratch_shapes=[
            pltpu.VMEM(down_w.shape, F32), pltpu.VMEM(up_w.shape, F32), dma((5,)),
        ],
        compiler_params=pltpu.CompilerParams(vmem_limit_bytes=58 * 1024 * 1024),
    )(*grads, first_sums, last_sums)


def solution(mesh):
    split = P("dp", "seq", None)
    return jax.shard_map(
        functools.partial(shards, mesh.shape["seq"], mesh.shape["dp"]),
        mesh=mesh,
        in_specs=(split,) * 5 + (P(), P()),
        out_specs=(split,) * 3 + (P(), P()),
        check_vma=False,
    )
```

time: 50.3 us -> 139 us (2.76)
  Pallas kernels: 41 us -> 138 us
  local copies, waits for them, and re-layouts: 8.3 us -> 0 us
    pallas_call x1, Pallas kernels: 1.89 us -> 97.4 us  [shards(): pl.pallas_call(functools.partial(finish, n_plane), out_shape=[jax.ShapeDt...]
    unnamed x14 -> x0, local copies, waits for them, and re-layouts: 8.3 us -> none
where the time goes in v3:
time: 139 us; the launch traced here: 138 us
  Pallas kernels  138 us (99%)
    pallas_call x1, Pallas kernels, shards(): pl.pallas_call(functools.partial(finish, n_plane), out_shape=[jax.ShapeDt...  97.4 us
    pallas_call x1, Pallas kernels, shards(): pl.pallas_call(functools.partial(kernel, n_seq, n_dp), out_shape=[jax.Sha...  40.4 us

profile of v3, /device:TPU:0, one launch (start us, length us, event | category | flops | bytes accessed | tf_op | source)
XLA Modules:
  0.0 138.5 jit_solution(5442027026822788863)
XLA Ops:
  0.6 40.4 %shard_map.110 = (bf16[1,256,2048]{2,1,0:T(8,128)(2,1)}, bf16[1,256,2048]{2,1,0:T(8,128)(2,1)}, bf16[1,256,2048]{2,1,0:T(8,128)(2,1)}, bf16[8,16,384]{2,1,0:T(8,128)(2,1)}, bf16[8,32,384]{2,1,0:T(8,128)(2,1)}) custom-call(bf16[1,256,4096]{2,1,0:T(8,128)(2,1)} %tok_hbm.1, bf16[1,256,2048]{2,1,0:T(8,128)(2,1)} %q_hbm.1, bf16[1,256,2048]{2,1,0:T(8,128)(2,1)} %k_hbm.1, ...), custom_call_target="tpu_custom_call" | custom-call | tf_op jit(solution)/shard_map/pallas_call | solution.py:302
  41.1 97.4 %shard_map.111 = (bf16[1,256,2048]{2,1,0:T(8,128)(2,1)}, bf16[1,256,2048]{2,1,0:T(8,128)(2,1)}, bf16[1,256,2048]{2,1,0:T(8,128)(2,1)}, f32[3,8,4096]{2,1,0:T(8,128)}, f32[3,8,2048]{2,1,0:T(8,128)}) custom-call(bf16[1,256,2048]{2,1,0:T(8,128)(2,1)} %get-tuple-element.10.gq_in, bf16[1,256,2048]{2,1,0:T(8,128)(2,1)} %get-tuple-element.11.gk_in, ...), custom_call_target="tpu_custom_call" | custom-call | tf_op jit(solution)/shard_map/pallas_call | solution.py:325

commit v4 on v3

--- a/solution.py
+++ b/solution.py
@@ -90,11 +90,15 @@
 
     upper, lower = pl.ds(half, half), pl.ds(0, half)
     shifted = pl.ds(half_width, half_width)
+    chunks = kv_send.shape[0] // 2
+    per = half_width // chunks
     kv_copies = [
         remote(
-            ref.at[0, upper, shifted], kv_in.at[i], kv_send.at[i], kv_recv.at[i],
-            {"seq": right, "dp": dp},
+            ref.at[0, upper, pl.ds(half_width + chunk * per, per)],
+            kv_in.at[i, :, pl.ds(chunk * per, per)],
+            kv_send.at[chunk * 2 + i], kv_recv.at[chunk * 2 + i], {"seq": right, "dp": dp},
         )
+        for chunk in range(chunks)
         for i, ref in enumerate((k_hbm, v_hbm))
     ]
     for copy in kv_copies:
@@ -123,13 +127,13 @@
         part[0, :, s] = dk
         part[1, :, s] = dv
 
-    for copy in kv_copies:
-        copy.wait_recv()
     ret_copies = []
-    chunks = ret_send.shape[0] // 2
-    per = heads // chunks
+    some = heads // chunks
     for chunk in range(chunks):
-        @pl.loop(chunk * per, (chunk + 1) * per, unroll=2)
+        for i in range(2):
+            kv_copies[chunk * 2 + i].wait_recv()
+
+        @pl.loop(chunk * some, (chunk + 1) * some, unroll=2)
         def _(h):
             c, s = cols(h + heads), cols(h)
             keys = jnp.concatenate([kv_in[0, :, s], k[0, lower, c]], axis=0)
@@ -141,7 +145,7 @@
             ret_out[0, :, s] = dk[:half].astype(BF16)
             ret_out[1, :, s] = dv[:half].astype(BF16)
 
-        span = pl.ds(chunk * per * HEAD_FEATURES, per * HEAD_FEATURES)
+        span = pl.ds(chunk * per, per)
         for i in range(2):
             at = chunk * 2 + i
             copy = remote(
@@ -260,12 +264,20 @@
         copy.wait_send()
 
 
-def finish(n_plane, gq_in, gk_in, gv_in, first, last_two, gq, gk, gv, gd, gu, down, up, sems):
+def finish(
+    n_plane, gq_in, gk_in, gv_in, first, last_two, gq, gk, gv, gd, gu, down, up, held, load_sem, sems
+):
+    loads = [
+        pltpu.make_async_copy(src, held.at[i], load_sem.at[i])
+        for i, src in enumerate((gq_in, gk_in, gv_in))
+    ]
     copies = [
-        pltpu.make_async_copy(src, dst, sems.at[i])
-        for i, (src, dst) in enumerate(((gq_in, gq), (gk_in, gk), (gv_in, gv)))
-    ]
-    for copy in copies:
+        pltpu.make_async_copy(held.at[i], dst, sems.at[i]) for i, dst in enumerate((gq, gk, gv))
+    ]
+    for copy in loads:
+        copy.start()
+    for load, copy in zip(loads, copies):
+        load.wait()
         copy.start()
     projections, ranks, model_width = down.shape
     wd, wu = model_width // n_plane, up.shape[2] // n_plane
@@ -316,7 +328,8 @@
             for piece in (first, last_two)
             for n in (n_plane, n_plane, n_z, n_plane)
         ]
-        + [dma((7,)), dma((3,)), dma((2,)), dma((2,)), dma((4,)), dma((4,))]
+        + [dma((7,)), dma((3,))]
+        + [dma((8,))] * 4
         + [dma((2, n)) for n in (n_plane, n_plane, n_z, n_z, n_plane, n_plane)],
         compiler_params=pltpu.CompilerParams(
             collective_id=0, has_side_effects=True, vmem_limit_bytes=58 * 1024 * 1024
@@ -329,7 +342,8 @@
         in_specs=[anywhere] * 3 + [vmem] * 2,
         out_specs=[anywhere] * 5,
         scratch_shapes=[
-            pltpu.VMEM(down_w.shape, F32), pltpu.VMEM(up_w.shape, F32), dma((5,)),
+            pltpu.VMEM(down_w.shape, F32), pltpu.VMEM(up_w.shape, F32),
+            pltpu.VMEM((3,) + query.shape, BF16), dma((3,)), dma((5,)),
         ],
         compiler_params=pltpu.CompilerParams(vmem_limit_bytes=58 * 1024 * 1024),
     )(*grads, first_sums, last_sums)

time: 139 us -> 43.3 us (0.31)
  Pallas kernels: 138 us -> 42.5 us
    pallas_call x1, Pallas kernels: 97.4 us -> 4.11 us  [shards(): pl.pallas_call(functools.partial(finish, n_plane), out_shape=[jax.ShapeDt...]
    pallas_call x1, Pallas kernels: 40.4 us -> 38.3 us  [shards(): pl.pallas_call(functools.partial(kernel, n_seq, n_dp), out_shape=[jax.Sha...]
where the time goes in v4:
time: 43.3 us; the launch traced here: 43.1 us
  Pallas kernels  42.5 us (98%)
  between operations  0.64 us (1%)
    pallas_call x1, Pallas kernels, shards(): pl.pallas_call(functools.partial(kernel, n_seq, n_dp), out_shape=[jax.Sha...  38.3 us
    pallas_call x1, Pallas kernels, shards(): pl.pallas_call(functools.partial(finish, n_plane), out_shape=[jax.ShapeDt...  4.11 us

profile of v4, /device:TPU:0, one launch (start us, length us, event | category | flops | bytes accessed | tf_op | source)
XLA Modules:
  0.0 43.1 jit_solution(16943866562505140580)
XLA Ops:
  0.6 38.3 %shard_map.110 = (bf16[1,256,2048]{2,1,0:T(8,128)(2,1)}, bf16[1,256,2048]{2,1,0:T(8,128)(2,1)}, bf16[1,256,2048]{2,1,0:T(8,128)(2,1)}, bf16[8,16,384]{2,1,0:T(8,128)(2,1)}, bf16[8,32,384]{2,1,0:T(8,128)(2,1)}) custom-call(bf16[1,256,4096]{2,1,0:T(8,128)(2,1)} %tok_hbm.1, bf16[1,256,2048]{2,1,0:T(8,128)(2,1)} %q_hbm.1, bf16[1,256,2048]{2,1,0:T(8,128)(2,1)} %k_hbm.1, ...), custom_call_target="tpu_custom_call" | custom-call | tf_op jit(solution)/shard_map/pallas_call | solution.py:314
  39.0 4.1 %shard_map.111 = (bf16[1,256,2048]{2,1,0:T(8,128)(2,1)}, bf16[1,256,2048]{2,1,0:T(8,128)(2,1)}, bf16[1,256,2048]{2,1,0:T(8,128)(2,1)}, f32[3,8,4096]{2,1,0:T(8,128)}, f32[3,8,2048]{2,1,0:T(8,128)}) custom-call(bf16[1,256,2048]{2,1,0:T(8,128)(2,1)} %get-tuple-element.10.gq_in, bf16[1,256,2048]{2,1,0:T(8,128)(2,1)} %get-tuple-element.11.gk_in, ...), custom_call_target="tpu_custom_call" | custom-call | tf_op jit(solution)/shard_map/pallas_call | solution.py:338

commit v5 on v4

--- a/solution.py
+++ b/solution.py
@@ -229,7 +229,9 @@
             remote(
                 gbuf.at[c], gbuf.at[c], ag_send.at[group, j], ag_recv.at[group, j], plane_id(j)[1]
             ).wait_recv()
-        out[...] = gbuf[...]
+        store = pltpu.make_async_copy(gbuf, out, store_sem.at[3 + group])
+        store.start()
+        stores.append(store)
 
     down_all = jnp.concatenate([down_w[p].astype(F32) for p in range(3)], axis=0).astype(BF16)
     projected = dot(down_all, tok[0], ((1,), (1,)))
@@ -265,7 +267,8 @@
 
 
 def finish(
-    n_plane, gq_in, gk_in, gv_in, first, last_two, gq, gk, gv, gd, gu, down, up, held, load_sem, sems
+    n_plane, gq_in, gk_in, gv_in, first_in, last_in, gq, gk, gv, gd, gu,
+    down, up, held, first, last_two, load_sem, sems
 ):
     loads = [
         pltpu.make_async_copy(src, held.at[i], load_sem.at[i])
@@ -274,11 +277,14 @@
     copies = [
         pltpu.make_async_copy(held.at[i], dst, sems.at[i]) for i, dst in enumerate((gq, gk, gv))
     ]
-    for copy in loads:
-        copy.start()
-    for load, copy in zip(loads, copies):
-        load.wait()
-        copy.start()
+    sum_loads = [
+        pltpu.make_async_copy(first_in, first, load_sem.at[3]),
+        pltpu.make_async_copy(last_in, last_two, load_sem.at[4]),
+    ]
+    for copy in sum_loads + loads:
+        copy.start()
+    for copy in sum_loads:
+        copy.wait()
     projections, ranks, model_width = down.shape
     wd, wu = model_width // n_plane, up.shape[2] // n_plane
     wide = (wd + wu) // 2
@@ -297,6 +303,9 @@
     ]
     for copy in last:
         copy.start()
+    for load, copy in zip(loads, copies):
+        load.wait()
+        copy.start()
     for copy in copies + last:
         copy.wait()
 
@@ -310,13 +319,12 @@
     first, last_two = (2 * ranks, across), (2 * (projections - 1) * ranks, across)
     dma = pltpu.SemaphoreType.DMA
     anywhere = pl.BlockSpec(memory_space=pl.ANY)
-    vmem = pl.BlockSpec(memory_space=pltpu.VMEM)
     *grads, first_sums, last_sums = pl.pallas_call(
         functools.partial(kernel, n_seq, n_dp),
         out_shape=[jax.ShapeDtypeStruct(query.shape, BF16)] * 3
         + [jax.ShapeDtypeStruct((n_plane,) + piece, BF16) for piece in (first, last_two)],
         in_specs=[anywhere] * 7,
-        out_specs=[anywhere] * 3 + [vmem] * 2,
+        out_specs=[anywhere] * 5,
         scratch_shapes=[
             pltpu.VMEM(ref.shape, BF16)
             for ref in (query, query, query, tokens, query, key, value, gradient, down_w, up_w)
@@ -328,7 +336,7 @@
             for piece in (first, last_two)
             for n in (n_plane, n_plane, n_z, n_plane)
         ]
-        + [dma((7,)), dma((3,))]
+        + [dma((7,)), dma((5,))]
         + [dma((8,))] * 4
         + [dma((2, n)) for n in (n_plane, n_plane, n_z, n_z, n_plane, n_plane)],
         compiler_params=pltpu.CompilerParams(
@@ -339,11 +347,13 @@
         functools.partial(finish, n_plane),
         out_shape=[jax.ShapeDtypeStruct(query.shape, BF16)] * 3
         + [jax.ShapeDtypeStruct(down_w.shape, F32), jax.ShapeDtypeStruct(up_w.shape, F32)],
-        in_specs=[anywhere] * 3 + [vmem] * 2,
+        in_specs=[anywhere] * 5,
         out_specs=[anywhere] * 5,
         scratch_shapes=[
             pltpu.VMEM(down_w.shape, F32), pltpu.VMEM(up_w.shape, F32),
-            pltpu.VMEM((3,) + query.shape, BF16), dma((3,)), dma((5,)),
+            pltpu.VMEM((3,) + query.shape, BF16),
+            pltpu.VMEM((n_plane,) + first, BF16), pltpu.VMEM((n_plane,) + last_two, BF16),
+            dma((5,)), dma((5,)),
         ],
         compiler_params=pltpu.CompilerParams(vmem_limit_bytes=58 * 1024 * 1024),
     )(*grads, first_sums, last_sums)

time: 43.3 us -> 42.4 us (0.979)
  Pallas kernels: 42.5 us -> 41.6 us
    pallas_call x1, Pallas kernels: 4.11 us -> 3.24 us  [shards(): pl.pallas_call(functools.partial(finish, n_plane), out_shape=[jax.ShapeDt...]
where the time goes in v5:
time: 42.4 us; the launch traced here: 42.2 us
  Pallas kernels  41.6 us (98%)
  between operations  0.64 us (2%)
    pallas_call x1, Pallas kernels, shards(): pl.pallas_call(functools.partial(kernel, n_seq, n_dp), out_shape=[jax.Sha...  38.3 us
    pallas_call x1, Pallas kernels, shards(): pl.pallas_call(functools.partial(finish, n_plane), out_shape=[jax.ShapeDt...  3.24 us

profile of v5, /device:TPU:0, one launch (start us, length us, event | category | flops | bytes accessed | tf_op | source)
XLA Modules:
  0.0 42.2 jit_solution(2517394412218375949)
XLA Ops:
  0.6 38.3 %shard_map.110 = (bf16[1,256,2048]{2,1,0:T(8,128)(2,1)}, bf16[1,256,2048]{2,1,0:T(8,128)(2,1)}, bf16[1,256,2048]{2,1,0:T(8,128)(2,1)}, bf16[8,16,384]{2,1,0:T(8,128)(2,1)}, bf16[8,32,384]{2,1,0:T(8,128)(2,1)}) custom-call(bf16[1,256,4096]{2,1,0:T(8,128)(2,1)} %tok_hbm.1, bf16[1,256,2048]{2,1,0:T(8,128)(2,1)} %q_hbm.1, bf16[1,256,2048]{2,1,0:T(8,128)(2,1)} %k_hbm.1, ...), custom_call_target="tpu_custom_call" | custom-call | tf_op jit(solution)/shard_map/pallas_call | solution.py:322
  38.9 3.2 %shard_map.111 = (bf16[1,256,2048]{2,1,0:T(8,128)(2,1)}, bf16[1,256,2048]{2,1,0:T(8,128)(2,1)}, bf16[1,256,2048]{2,1,0:T(8,128)(2,1)}, f32[3,8,4096]{2,1,0:T(8,128)}, f32[3,8,2048]{2,1,0:T(8,128)}) custom-call(bf16[1,256,2048]{2,1,0:T(8,128)(2,1)} %get-tuple-element.10.gq_in, bf16[1,256,2048]{2,1,0:T(8,128)(2,1)} %get-tuple-element.11.gk_in, ...), custom_call_target="tpu_custom_call" | custom-call | tf_op jit(solution)/shard_map/pallas_call | solution.py:346
